TPU v7x, 32 devices: a whole 2x2x4 slice. The times are simulated.
32 devices in a mesh: ev: 32 (over z, y, x, core).
Axes of the slice: x: 2, y: 2, z: 4, core: 2. Of those that a mesh axis runs over, the one named last changes fastest.
Arguments:
- records: bfloat16 [4096, 512], P('ev'), may hold values from -16 to 16
- filter_taps: bfloat16 [65], replicated, may hold values from -0.75 to 0.75
- live_counts: int32 [32], P('ev'), may hold values from 64 to 128, as said below
- pair_valid: int32 [32, 9], P('ev'), may hold values 0 or 1
Outputs:
- correlations: bfloat16 [4096, 10, 25, 128], P('ev')
Inputs may be any that keep to these rules, and one draw needn't show every extreme that they name: The first live_counts[b] events of block b are live and its other rows are padding; some block has all 128 events live.
All inputs are finite; a program needn't handle non-finite values. No bound on the sum of `pair_valid` on one device may be relied on, other than what follows from the above.
Results may differ from a plain program's by a relative error of at most 0.0047.
Values may be sent and summed in bfloat16 or wider, within the bound.
A program may use at most 64 MiB of HBM per device.

v0:
```python
import jax
import jax.numpy as jnp
from jax import lax
from jax.sharding import PartitionSpec as P

HALF = 12


epsilon = 1e-06


def passed_along(block, axis, distance):
    devices = range(lax.axis_size(axis))
    route = [(i - distance, i) for i in devices if i - distance in devices]
    return lax.ppermute(block, axis, route)


def band_matrix(filter_taps, samples):
    half_taps = (filter_taps.shape[0] - 1) // 2
    period = 2 * samples - 1
    spread = jnp.zeros((period,), jnp.float32)
    spread = lax.dynamic_update_slice(
        spread, filter_taps.astype(jnp.float32), (samples - 1 - half_taps,)
    )
    repeated = jnp.tile(spread, samples + 1)[: samples * (period + 1)]
    hankel = repeated.reshape(samples, period + 1)[:, :samples]
    return hankel[:, ::-1].astype(jnp.bfloat16)


def correlate_all(own_block, own_scale, stacked_partners, weights):
    count, events, samples = stacked_partners.shape
    partner_scale = lax.rsqrt(
        jnp.sum(jnp.square(stacked_partners.astype(jnp.float32)), axis=2) + epsilon
    )
    flat = stacked_partners.reshape(count * events, samples)
    own_padded = jnp.pad(own_block, ((0, 0), (HALF, HALF)))
    products = []
    for lag_index in range(2 * HALF + 1):
        start = 2 * HALF - lag_index
        shifted_own = own_padded[:, start : start + samples]
        product = lax.dot_general(
            shifted_own, flat, (((1,), (1,)), ((), ())), preferred_element_type=jnp.float32
        )
        products.append(product.reshape(events, count, events))
    stacked = jnp.stack(products, axis=2)
    scaled = (
        stacked
        * own_scale[:, None, None, None]
        * partner_scale[None, :, None, :]
        * weights[None, :, None, None]
    )
    return scaled.astype(jnp.bfloat16)


def shards(records, filter_taps, live_counts, pair_valid):
    events, samples = records.shape
    partner_count = pair_valid.shape[1]
    row_index = lax.broadcasted_iota(jnp.int32, (events, 1), 0)
    kept_rows = jnp.where(row_index < live_counts[0], records, jnp.zeros((), records.dtype))
    matrix = band_matrix(filter_taps, samples)

    def smooth(block):
        return jnp.dot(block, matrix, preferred_element_type=jnp.float32).astype(jnp.bfloat16)

    own_block = smooth(kept_rows)
    own_scale = lax.rsqrt(jnp.sum(jnp.square(own_block.astype(jnp.float32)), axis=1) + epsilon)
    partners = []
    for distance in range(1, partner_count + 1):
        partners.append(passed_along(kept_rows, "ev", -distance))
    received = jnp.stack(partners, axis=0)
    smoothed = smooth(received.reshape(partner_count * events, samples)).reshape(
        partner_count, events, samples
    )
    stacked_partners = jnp.concatenate([own_block[None], smoothed], axis=0)
    weights = jnp.concatenate(
        [jnp.ones((1,), jnp.float32), pair_valid[0].astype(jnp.float32)], axis=0
    )
    return correlate_all(own_block, own_scale, stacked_partners, weights)


def solution(mesh):
    in_specs = (P("ev", None), P(), P("ev"), P("ev", None))
    out_specs = P("ev", None, None, None)
    return jax.shard_map(shards, mesh=mesh, in_specs=in_specs, out_specs=out_specs, check_vma=False)
```

profile of v0, /device:TPU:15, one launch (start us, length us, event | category | flops | bytes accessed | tf_op | source)
XLA Modules:
  0.0 62.2 jit_solution(13607199458630952377)
XLA Ops:
  0.7 1.0 %broadcast_select_fusion = bf16[128,512]{1,0:T(8,128)(2,1)S(1)} fusion(bf16[128,512]{1,0:T(8,128)(2,1)} %param.4, pred[128]{0:T(512)(128)(4,1)S(1)} %iota_compare_fusion), kind=kLoop, calls=%fused_computation.116 | loop fusion | flops 65536 | bytes 262272 | tf_op jit(solution)/shard_map/jit(_where)/select_n | solution.py:59
  1.7 2.6 %collective-permute-start = (bf16[128,512]{1,0:T(8,128)(2,1)S(1)}, bf16[128,512]{1,0:T(8,128)(2,1)S(1)}, u32[]{:S(2)}, u32[]{:S(2)}) collective-permute-start(bf16[128,512]{1,0:T(8,128)(2,1)S(1)} %broadcast_select_fusion), channel_id=1, source_target_pairs={{1,0},{2,1},{3,2},{4,3},{5,4},{6,5},{7,6},{8,7},{9,8},{10,9},{11,1... | collective-permute-start | bytes 393224 | tf_op jit(solution)/shard_map/ppermute | solution.py:15
  4.3 2.2 %collective-permute-start.1 = (bf16[128,512]{1,0:T(8,128)(2,1)S(1)}, bf16[128,512]{1,0:T(8,128)(2,1)S(1)}, u32[]{:S(2)}, u32[]{:S(2)}) collective-permute-start(bf16[128,512]{1,0:T(8,128)(2,1)S(1)} %broadcast_select_fusion), channel_id=1, source_target_pairs={{2,0},{3,1},{4,2},{5,3},{6,4},{7,5},{8,6},{9,7},{10,8},{11,9},{12,... | collective-permute-start | bytes 393224 | tf_op jit(solution)/shard_map/ppermute | solution.py:15
  6.4 3.2 %collective-permute-start.2 = (bf16[128,512]{1,0:T(8,128)(2,1)S(1)}, bf16[128,512]{1,0:T(8,128)(2,1)S(1)}, u32[]{:S(2)}, u32[]{:S(2)}) collective-permute-start(bf16[128,512]{1,0:T(8,128)(2,1)S(1)} %broadcast_select_fusion), channel_id=1, source_target_pairs={{3,0},{4,1},{5,2},{6,3},{7,4},{8,5},{9,6},{10,7},{11,8},{12,9},{13... | collective-permute-start | bytes 393224 | tf_op jit(solution)/shard_map/ppermute | solution.py:15
  9.7 3.0 %collective-permute-start.3 = (bf16[128,512]{1,0:T(8,128)(2,1)S(1)}, bf16[128,512]{1,0:T(8,128)(2,1)S(1)}, u32[]{:S(2)}, u32[]{:S(2)}) collective-permute-start(bf16[128,512]{1,0:T(8,128)(2,1)S(1)} %broadcast_select_fusion), channel_id=1, source_target_pairs={{4,0},{5,1},{6,2},{7,3},{8,4},{9,5},{10,6},{11,7},{12,8},{13,9},{1... | collective-permute-start | bytes 393224 | tf_op jit(solution)/shard_map/ppermute | solution.py:15
  12.7 2.1 %collective-permute-start.4 = (bf16[128,512]{1,0:T(8,128)(2,1)S(1)}, bf16[128,512]{1,0:T(8,128)(2,1)S(1)}, u32[]{:S(2)}, u32[]{:S(2)}) collective-permute-start(bf16[128,512]{1,0:T(8,128)(2,1)S(1)} %broadcast_select_fusion), channel_id=1, source_target_pairs={{5,0},{6,1},{7,2},{8,3},{9,4},{10,5},{11,6},{12,7},{13,8},{14,9},{... | collective-permute-start | bytes 393224 | tf_op jit(solution)/shard_map/ppermute | solution.py:15
  14.9 0.7 %pad_convert_fusion = bf16[1023]{0:T(1024)(128)(2,1)S(1)} fusion(bf16[65]{0:T(256)(128)(2,1)} %param.5), kind=kLoop, calls=%fused_computation.142 | loop fusion | bytes 2176 | tf_op jit(solution)/shard_map/dynamic_update_slice | solution.py:22
  15.6 0.1 tile.4
  15.7 1.6 %tile.10 = bf16[524799]{0:T(1024)(128)(2,1)S(1)} reshape(bf16[513,1023]{1,0:T(8,128)(2,1)S(1)} %tile.4) | data formatting | bytes 2099196 | tf_op jit(solution)/shard_map/tile | solution.py:25
  17.4 0.5 reshape.151
  18.0 1.6 %rev.3 = bf16[512,512]{1,0:T(8,128)(2,1)S(1)} reverse(bf16[512,512]{1,0:T(8,128)(2,1)S(1)} %slice.106), dimensions={1} | reverse | bytes 1048576 | tf_op jit(solution)/shard_map/rev | solution.py:27
  19.6 0.3 multiply_reduce_fusion.1
  20.1 2.5 %collective-permute-start.5 = (bf16[128,512]{1,0:T(8,128)(2,1)S(1)}, bf16[128,512]{1,0:T(8,128)(2,1)S(1)}, u32[]{:S(2)}, u32[]{:S(2)}) collective-permute-start(bf16[128,512]{1,0:T(8,128)(2,1)S(1)} %broadcast_select_fusion), channel_id=1, source_target_pairs={{6,0},{7,1},{8,2},{9,3},{10,4},{11,5},{12,6},{13,7},{14,8},{15,9},... | collective-permute-start | bytes 393224 | tf_op jit(solution)/shard_map/ppermute | solution.py:15
  22.6 1.9 %collective-permute-start.6 = (bf16[128,512]{1,0:T(8,128)(2,1)S(1)}, bf16[128,512]{1,0:T(8,128)(2,1)S(1)}, u32[]{:S(2)}, u32[]{:S(2)}) collective-permute-start(bf16[128,512]{1,0:T(8,128)(2,1)S(1)} %broadcast_select_fusion), channel_id=1, source_target_pairs={{7,0},{8,1},{9,2},{10,3},{11,4},{12,5},{13,6},{14,7},{15,8},{16,9}... | collective-permute-start | bytes 393224 | tf_op jit(solution)/shard_map/ppermute | solution.py:15
  24.6 1.9 %collective-permute-start.7 = (bf16[128,512]{1,0:T(8,128)(2,1)S(1)}, bf16[128,512]{1,0:T(8,128)(2,1)S(1)}, u32[]{:S(2)}, u32[]{:S(2)}) collective-permute-start(bf16[128,512]{1,0:T(8,128)(2,1)S(1)} %broadcast_select_fusion), channel_id=1, source_target_pairs={{8,0},{9,1},{10,2},{11,3},{12,4},{13,5},{14,6},{15,7},{16,8},{17,9... | collective-permute-start | bytes 393224 | tf_op jit(solution)/shard_map/ppermute | solution.py:15
  26.6 2.1 %collective-permute-start.8 = (bf16[128,512]{1,0:T(8,128)(2,1)S(1)}, bf16[128,512]{1,0:T(8,128)(2,1)S(1)}, u32[]{:S(2)}, u32[]{:S(2)}) collective-permute-start(bf16[128,512]{1,0:T(8,128)(2,1)S(1)} %broadcast_select_fusion), channel_id=1, source_target_pairs={{9,0},{10,1},{11,2},{12,3},{13,4},{14,5},{15,6},{16,7},{17,8},{18,... | collective-permute-start | bytes 393224 | tf_op jit(solution)/shard_map/ppermute | solution.py:15
  28.7 1.4 %collective-permute-done.6 = bf16[128,512]{1,0:T(8,128)(2,1)S(1)} collective-permute-done((bf16[128,512]{1,0:T(8,128)(2,1)S(1)}, bf16[128,512]{1,0:T(8,128)(2,1)S(1)}, u32[]{:S(2)}, u32[]{:S(2)}) %collective-permute-start.6) | collective-permute-done | bytes 131104 | tf_op jit(solution)/shard_map/ppermute | solution.py:15
  30.2 2.3 %collective-permute-done.7 = bf16[128,512]{1,0:T(8,128)(2,1)S(1)} collective-permute-done((bf16[128,512]{1,0:T(8,128)(2,1)S(1)}, bf16[128,512]{1,0:T(8,128)(2,1)S(1)}, u32[]{:S(2)}, u32[]{:S(2)}) %collective-permute-start.7) | collective-permute-done | bytes 131104 | tf_op jit(solution)/shard_map/ppermute | solution.py:15
  32.5 6.1 %collective-permute-done.8 = bf16[128,512]{1,0:T(8,128)(2,1)S(1)} collective-permute-done((bf16[128,512]{1,0:T(8,128)(2,1)S(1)}, bf16[128,512]{1,0:T(8,128)(2,1)S(1)}, u32[]{:S(2)}, u32[]{:S(2)}) %collective-permute-start.8) | collective-permute-done | bytes 131104 | tf_op jit(solution)/shard_map/ppermute | solution.py:15
  38.7 0.8 %convolution_convert_fusion = bf16[1152,512]{1,0:T(8,128)(2,1)S(1)} fusion(bf16[1152,512]{1,0:T(8,128)(2,1)S(1)} %bitcast.256, bf16[512,512]{1,0:T(8,128)(2,1)S(1)} %rev.3), kind=kOutput, calls=%fused_computation.1 | convolution fusion | flops 604569600 | bytes 2883584 | tf_op jit(solution)/shard_map/dot_general | solution.py:63
  39.4 0.6 fusion.24
  40.0 0.3 multiply_reduce_fusion
  40.3 0.6 fusion.23
  40.9 0.6 fusion.22
  41.5 0.6 fusion.21
  42.0 0.6 fusion.20
  42.6 0.6 fusion.19
  43.2 0.6 fusion.18
  43.7 0.6 fusion.17
  44.3 0.6 fusion.16
  44.8 0.6 fusion.15
  45.4 0.6 fusion.14
  46.0 0.6 fusion.13
  46.5 0.5 fusion.12
  47.1 0.6 fusion.11
  47.7 0.6 fusion.10
  48.2 0.6 fusion.9
  48.8 0.6 fusion.8
  49.4 0.6 fusion.7
  49.9 0.6 fusion.6
  50.5 0.6 fusion.5
  51.0 0.6 fusion.4
  51.6 0.6 fusion.3
  52.2 0.6 fusion.2
  52.7 0.6 fusion.1
  53.3 0.6 fusion
  53.9 3.2 %multiply_convert_fusion = bf16[128,10,25,128]{3,0,1,2:T(8,128)(2,1)S(1)} fusion(f32[128,10,25,128]{3,0,1,2:T(8,128)S(1)} %fusion, f32[10]{0:T(128)S(1)} %pad_maximum_fusion.1, f32[10,128]{1,0:T(8,128)S(1)} %add_rsqrt_fusion, f32[128]{0:T(128)S(1)} %add_rsqrt_fusion.1), kind=kLoop, calls=%fused_computation | loop fusion | flops 16384000 | bytes 24581672 | tf_op jit(solution)/shard_map/convert_element_type | solution.py:52
  57.1 5.2 %copy.5 = bf16[128,10,25,128]{3,0,2,1:T(8,128)(2,1)} copy(bf16[128,10,25,128]{3,0,1,2:T(8,128)(2,1)S(1)} %multiply_convert_fusion) | data formatting | bytes 16384000 | tf_op jit(solution)/shard_map/convert_element_type | solution.py:52
  (24 shorter events, 0.3 us)
Async XLA Ops:
  1.7 18.4 %collective-permute-start = (bf16[128,512]{1,0:T(8,128)(2,1)S(1)}, bf16[128,512]{1,0:T(8,128)(2,1)S(1)}, u32[]{:S(2)}, u32[]{:S(2)}) collective-permute-start(bf16[128,512]{1,0:T(8,128)(2,1)S(1)} %broadcast_select_fusion), channel_id=1, source_target_pairs={{1,0},{2,1},{3,2},{4,3},{5,4},{6,5},{7,6},{8,7},{9,8},{10,9},{11,1... | collective-permute-start | bytes 393224 | tf_op jit(solution)/shard_map/ppermute | solution.py:15
  4.3 18.4 %collective-permute-start.1 = (bf16[128,512]{1,0:T(8,128)(2,1)S(1)}, bf16[128,512]{1,0:T(8,128)(2,1)S(1)}, u32[]{:S(2)}, u32[]{:S(2)}) collective-permute-start(bf16[128,512]{1,0:T(8,128)(2,1)S(1)} %broadcast_select_fusion), channel_id=1, source_target_pairs={{2,0},{3,1},{4,2},{5,3},{6,4},{7,5},{8,6},{9,7},{10,8},{11,9},{12,... | collective-permute-start | bytes 393224 | tf_op jit(solution)/shard_map/ppermute | solution.py:15
  6.4 18.2 %collective-permute-start.2 = (bf16[128,512]{1,0:T(8,128)(2,1)S(1)}, bf16[128,512]{1,0:T(8,128)(2,1)S(1)}, u32[]{:S(2)}, u32[]{:S(2)}) collective-permute-start(bf16[128,512]{1,0:T(8,128)(2,1)S(1)} %broadcast_select_fusion), channel_id=1, source_target_pairs={{3,0},{4,1},{5,2},{6,3},{7,4},{8,5},{9,6},{10,7},{11,8},{12,9},{13... | collective-permute-start | bytes 393224 | tf_op jit(solution)/shard_map/ppermute | solution.py:15
  9.7 16.9 %collective-permute-start.3 = (bf16[128,512]{1,0:T(8,128)(2,1)S(1)}, bf16[128,512]{1,0:T(8,128)(2,1)S(1)}, u32[]{:S(2)}, u32[]{:S(2)}) collective-permute-start(bf16[128,512]{1,0:T(8,128)(2,1)S(1)} %broadcast_select_fusion), channel_id=1, source_target_pairs={{4,0},{5,1},{6,2},{7,3},{8,4},{9,5},{10,6},{11,7},{12,8},{13,9},{1... | collective-permute-start | bytes 393224 | tf_op jit(solution)/shard_map/ppermute | solution.py:15
  12.7 16.0 %collective-permute-start.4 = (bf16[128,512]{1,0:T(8,128)(2,1)S(1)}, bf16[128,512]{1,0:T(8,128)(2,1)S(1)}, u32[]{:S(2)}, u32[]{:S(2)}) collective-permute-start(bf16[128,512]{1,0:T(8,128)(2,1)S(1)} %broadcast_select_fusion), channel_id=1, source_target_pairs={{5,0},{6,1},{7,2},{8,3},{9,4},{10,5},{11,6},{12,7},{13,8},{14,9},{... | collective-permute-start | bytes 393224 | tf_op jit(solution)/shard_map/ppermute | solution.py:15
  17.9 2.0 %copy-start = (s32[1,9]{1,0:T(1,128)S(1)}, s32[1,9]{1,0:T(1,128)}, u32[]{:S(2)}) copy-start(s32[1,9]{1,0:T(1,128)} %param.7) | copy-start | bytes 112
  20.1 8.6 %collective-permute-start.5 = (bf16[128,512]{1,0:T(8,128)(2,1)S(1)}, bf16[128,512]{1,0:T(8,128)(2,1)S(1)}, u32[]{:S(2)}, u32[]{:S(2)}) collective-permute-start(bf16[128,512]{1,0:T(8,128)(2,1)S(1)} %broadcast_select_fusion), channel_id=1, source_target_pairs={{6,0},{7,1},{8,2},{9,3},{10,4},{11,5},{12,6},{13,7},{14,8},{15,9},... | collective-permute-start | bytes 393224 | tf_op jit(solution)/shard_map/ppermute | solution.py:15
  22.6 7.5 %collective-permute-start.6 = (bf16[128,512]{1,0:T(8,128)(2,1)S(1)}, bf16[128,512]{1,0:T(8,128)(2,1)S(1)}, u32[]{:S(2)}, u32[]{:S(2)}) collective-permute-start(bf16[128,512]{1,0:T(8,128)(2,1)S(1)} %broadcast_select_fusion), channel_id=1, source_target_pairs={{7,0},{8,1},{9,2},{10,3},{11,4},{12,5},{13,6},{14,7},{15,8},{16,9}... | collective-permute-start | bytes 393224 | tf_op jit(solution)/shard_map/ppermute | solution.py:15
  24.6 7.9 %collective-permute-start.7 = (bf16[128,512]{1,0:T(8,128)(2,1)S(1)}, bf16[128,512]{1,0:T(8,128)(2,1)S(1)}, u32[]{:S(2)}, u32[]{:S(2)}) collective-permute-start(bf16[128,512]{1,0:T(8,128)(2,1)S(1)} %broadcast_select_fusion), channel_id=1, source_target_pairs={{8,0},{9,1},{10,2},{11,3},{12,4},{13,5},{14,6},{15,7},{16,8},{17,9... | collective-permute-start | bytes 393224 | tf_op jit(solution)/shard_map/ppermute | solution.py:15
  26.6 12.1 %collective-permute-start.8 = (bf16[128,512]{1,0:T(8,128)(2,1)S(1)}, bf16[128,512]{1,0:T(8,128)(2,1)S(1)}, u32[]{:S(2)}, u32[]{:S(2)}) collective-permute-start(bf16[128,512]{1,0:T(8,128)(2,1)S(1)} %broadcast_select_fusion), channel_id=1, source_target_pairs={{9,0},{10,1},{11,2},{12,3},{13,4},{14,5},{15,6},{16,7},{17,8},{18,... | collective-permute-start | bytes 393224 | tf_op jit(solution)/shard_map/ppermute | solution.py:15
where the time goes:
time: 62.6 us; the launch traced here: 62.2 us
  starting transfers between devices  21.6 us (35%)
  matrix products  15 us (24%)
  local copies, waits for them, and re-layouts  10 us (16%)
  waiting for transfers between devices  9.89 us (16%)
  other arithmetic  4.59 us (7%)
  between operations  1.13 us (2%)
    ppermute x9, starting transfers between devices, passed_along(): return lax.ppermute(block, axis, route)  21.6 us
    dot_general x25, matrix products, correlate_all(): lax.dot_general(shifted_own, flat, (((1,), (1,)), ((), ())), preferred_el...  13.9 us
    ppermute x9, waiting for transfers between devices, passed_along(): return lax.ppermute(block, axis, route)  9.89 us
    convert_element_type x1, local copies, waits for them, and re-layouts, correlate_all(): return scaled.astype(jnp.bfloat16)  5.18 us
    convert_element_type x1, other arithmetic, correlate_all(): return scaled.astype(jnp.bfloat16)  3.18 us
    another operation x2, local copies, waits for them, and re-layouts, band_matrix(): repeated = jnp.tile(spread, samples + 1)[:samples * (period + 1)]  1.75 us
    rev x1, local copies, waits for them, and re-layouts, band_matrix(): return hankel[:, ::-1].astype(jnp.bfloat16)  1.65 us
  transfers between devices with their start and end apart: 9, of which 3 were waited for; matrix products, arithmetic and copies ran while one was open for 8% of the time, Pallas kernels for 0%

commit v1 on v0

v1 whole, which is shorter than its diff:
```python
import functools

import jax
import jax.numpy as jnp
from jax import lax
from jax.experimental import pallas as pl
from jax.experimental.pallas import tpu as pltpu
from jax.sharding import PartitionSpec as P

HALF = 12
LAGS = 2 * HALF + 1
LAGS_AT_ONCE = 5
LANES = 128

epsilon = 1e-06

NT = (((1,), (1,)), ((), ()))
NN = (((1,), (0,)), ((), ()))


def split_squares(block):
    wide = block.astype(jnp.float32)
    square = wide * wide
    high = square.astype(jnp.bfloat16)
    low = (square - high.astype(jnp.float32)).astype(jnp.bfloat16)
    return high, low


def kernel(
    devices, records, taps, live_count, pair_valid, out,
    held, shifted, spread, row_scale, scale,
    z_sem, layer_sem, ten_sem, pair_sem, recv_sem,
):
    events, samples = records.shape
    reach = pair_valid.shape[1]
    half_taps = (taps.shape[1] - 1) // 2
    per_layer = (reach - 1) // 2
    far = reach - 1
    last = reach + 1
    chips = devices // 2
    me = lax.axis_index("ev")
    core = lax.rem(me, 2)
    chip = me // 2
    place = lax.rem(chip, per_layer)
    sibling = me + 1 - 2 * core

    def in_layer(d):
        return me - 2 * place + 2 * lax.rem(place + per_layer - d, per_layer)

    barrier = pltpu.get_barrier_semaphore()

    def greet(device):
        pl.semaphore_signal(
            barrier, inc=1, device_id=(device,), device_id_type=pl.DeviceIdType.MESH
        )

    has_down = chip >= per_layer
    has_up = chip + per_layer < chips
    down_edge = (core == 0) & (place == 0) & (chip >= 1)
    up_edge = (core == 0) & (place == per_layer - 1) & (chip + 1 < chips)
    greet(sibling)
    for d in range(1, per_layer):
        greet(in_layer(d))

    @pl.when(has_down)
    def _():
        greet(me - 2 * per_layer)

    @pl.when(has_up)
    def _():
        greet(me + 2 * per_layer)

    @pl.when(down_edge)
    def _():
        greet(me - 2)

    @pl.when(up_edge)
    def _():
        greet(me + 2)

    spread[...] = jnp.zeros_like(spread)
    spread[0:1, 0 : taps.shape[1]] = taps[...].astype(jnp.float32)
    rolled = pltpu.roll(
        jnp.broadcast_to(spread[0:1, :], (samples, samples)),
        samples - half_taps, 1, stride=1, stride_axis=0,
    )
    t = lax.broadcasted_iota(jnp.int32, (samples, samples), 0)
    u = lax.broadcasted_iota(jnp.int32, (samples, samples), 1)
    band = jnp.where(jnp.abs(u - t) <= half_taps, rolled, 0.0).astype(jnp.bfloat16)
    row = lax.broadcasted_iota(jnp.int32, (events, samples), 0)
    kept = jnp.where(row < live_count[0], records[...].astype(jnp.float32), 0.0)
    own = lax.dot_general(
        kept.astype(jnp.bfloat16), band, NT, preferred_element_type=jnp.float32
    ).astype(jnp.bfloat16)
    held[0] = own

    for k in range(1, last + 1):
        if k == last:
            missing = (core == 0) & (me + k >= devices)
        else:
            missing = me + k >= devices

        @pl.when(missing)
        def _(k=k):
            held[k] = jnp.zeros((events, samples), jnp.bfloat16)

    greeted = (
        per_layer
        + has_down.astype(jnp.int32)
        + has_up.astype(jnp.int32)
        + down_edge.astype(jnp.int32)
        + up_edge.astype(jnp.int32)
    )
    pl.semaphore_wait(barrier, greeted)

    def remote(source, slot, send_sem, device):
        return pltpu.make_async_remote_copy(
            src_ref=held.at[source],
            dst_ref=held.at[slot],
            send_sem=send_sem,
            recv_sem=recv_sem.at[slot],
            device_id=(device,),
            device_id_type=pl.DeviceIdType.MESH,
        )

    def arrived(slot):
        remote(slot, slot, z_sem, sibling).wait_recv()

    def to_sibling(i):
        return remote(2 * i + 2 - 2 * core, 2 * i + 1, pair_sem.at[i], sibling)

    def sibling_wants(i):
        return 2 * chip + 2 * i + 2 - 2 * core < devices

    def z_copy():
        return remote(0, far, z_sem, me - 2 * per_layer)

    def layer_copy(d, source):
        return remote(source, 2 * d, layer_sem.at[d - 1], in_layer(d))

    def ten_copy():
        return remote(far, last, ten_sem, me - 2)

    @pl.when(has_down)
    def _():
        z_copy().start()

    for d in range(per_layer - 1, 0, -1):
        @pl.when(place >= d)
        def _(d=d):
            layer_copy(d, 0).start()

    @pl.when(core == 1)
    def _():
        to_sibling(0).start()

    padded = jnp.concatenate(
        [own.astype(jnp.float32), jnp.zeros((events, LANES), jnp.float32)], axis=1
    )
    width = samples + LANES
    for lag in range(LAGS):
        moved = pltpu.roll(padded, (lag - HALF) % width, 1) if lag != HALF else padded
        shifted[lag] = moved[:, :samples].astype(jnp.bfloat16)
    ones = jnp.ones((samples, LANES), jnp.bfloat16)
    high, low = split_squares(own)
    row_scale[...] = lax.rsqrt(
        lax.dot_general(high, ones, NN, preferred_element_type=jnp.float32)
        + lax.dot_general(low, ones, NN, preferred_element_type=jnp.float32)
        + epsilon
    )

    def pass_far():
        @pl.when(has_up)
        def _():
            arrived(far)
            for d in range(per_layer - 1, 0, -1):
                @pl.when(place < d)
                def _(d=d):
                    layer_copy(d, far).start()

            @pl.when((core == 0) & (chip >= 1))
            def _():
                ten_copy().start()

            @pl.when(core == 0)
            def _():
                to_sibling(far // 2 - 1).start()

            @pl.when(core == 1)
            def _():
                to_sibling(far // 2).start()

    def pass_on(slot):
        @pl.when(2 * chip + slot < devices)
        def _():
            arrived(slot)

            @pl.when(core == 0)
            def _():
                to_sibling(slot // 2 - 1).start()

            @pl.when(core == 1)
            def _():
                to_sibling(slot // 2).start()

    def pass_last():
        @pl.when((core == 0) & (me + last < devices))
        def _():
            arrived(last)
            to_sibling(last // 2 - 1).start()

    def receive(slot):
        @pl.when(me + slot < devices)
        def _():
            arrived(slot)

    def correlate(slots):
        for i, slot in enumerate(slots):
            high, low = split_squares(held[slot])
            rows = jnp.ones((8, samples), jnp.bfloat16)
            total = lax.dot_general(rows, high, NT, preferred_element_type=jnp.float32)
            total += lax.dot_general(rows, low, NT, preferred_element_type=jnp.float32)
            partner_scale = lax.rsqrt(total + epsilon)
            if slot > 0:
                partner_scale *= pair_valid[0, slot - 1].astype(jnp.float32)
            scale[:, i * events : (i + 1) * events] = row_scale[...] * partner_scale[0:1, :]

        def some_lags(c, carry):
            lags = pl.ds(c * LAGS_AT_ONCE, LAGS_AT_ONCE)
            left = shifted[lags].reshape(LAGS_AT_ONCE * events, samples)
            right = jnp.concatenate([held[slot] for slot in slots], axis=0)
            product = lax.dot_general(left, right, NT, preferred_element_type=jnp.float32)
            product = product.reshape(LAGS_AT_ONCE, events, len(slots) * events)
            product = (product * scale[...][None]).astype(jnp.bfloat16)
            for i, slot in enumerate(slots):
                out[slot, lags] = product[:, :, i * events : (i + 1) * events]
            return carry

        lax.fori_loop(0, LAGS // LAGS_AT_ONCE, some_lags, 0)

    pass_far()
    correlate((0, far))
    evens = list(range(2, far, 2))
    ready = []
    for slot in evens:
        pass_on(slot)
        ready.append(slot)
        if len(ready) == 2:
            correlate(tuple(ready))
            ready = []
    pass_last()
    for slot in range(1, reach + 1, 2):
        receive(slot)
        ready.append(slot)
        if len(ready) == 2:
            correlate(tuple(ready))
            ready = []

    @pl.when(has_down)
    def _():
        z_copy().wait_send()

    for d in range(1, per_layer):
        @pl.when((place >= d) | has_up)
        def _(d=d):
            layer_copy(d, 0).wait_send()

    @pl.when((core == 0) & (chip >= 1) & has_up)
    def _():
        ten_copy().wait_send()

    for i in range((reach + 1) // 2):
        @pl.when(sibling_wants(i))
        def _(i=i):
            to_sibling(i).wait_send()


def shards(devices, records, filter_taps, live_counts, pair_valid):
    events, samples = records.shape
    reach = pair_valid.shape[1]
    vmem = pl.BlockSpec(memory_space=pltpu.VMEM)
    smem = pl.BlockSpec(memory_space=pltpu.SMEM)
    correlations = pl.pallas_call(
        functools.partial(kernel, devices),
        out_shape=pltpu.VMEM((reach + 1, LAGS, events, events), jnp.bfloat16),
        in_specs=[vmem, vmem, smem, smem],
        out_specs=vmem,
        scratch_shapes=[
            pltpu.VMEM((reach + 2, events, samples), jnp.bfloat16),
            pltpu.VMEM((LAGS, events, samples), jnp.bfloat16),
            pltpu.VMEM((8, samples), jnp.float32),
            pltpu.VMEM((events, LANES), jnp.float32),
            pltpu.VMEM((events, 2 * events), jnp.float32),
            pltpu.SemaphoreType.DMA,
            pltpu.SemaphoreType.DMA(((reach - 1) // 2 - 1,)),
            pltpu.SemaphoreType.DMA,
            pltpu.SemaphoreType.DMA(((reach + 1) // 2,)),
            pltpu.SemaphoreType.DMA((reach + 2,)),
        ],
        compiler_params=pltpu.CompilerParams(
            collective_id=0, has_side_effects=True, vmem_limit_bytes=40 * 1024 * 1024
        ),
        cost_estimate=pl.CostEstimate(
            flops=2 * (reach + 1) * LAGS * events * events * samples,
            bytes_accessed=2 * (reach + 1) * LAGS * events * events,
            transcendentals=0,
        ),
    )(records, filter_taps.reshape(1, -1), live_counts, pair_valid)
    return jnp.transpose(correlations, (2, 0, 1, 3))


def solution(mesh):
    in_specs = (P("ev", None), P(), P("ev"), P("ev", None))
    out_specs = P("ev", None, None, None)
    return jax.shard_map(
        functools.partial(shards, mesh.shape["ev"]),
        mesh=mesh, in_specs=in_specs, out_specs=out_specs, check_vma=False,
    )
```

time: 62.6 us -> 30.2 us (0.48)
  the two profiles are of different devices: /device:TPU:15 before, /device:TPU:14 now
where the time goes in v1:
time: 30.2 us; the launch traced here: 30.1 us
  Pallas kernels  23.8 us (79%)
  local copies, waits for them, and re-layouts  5.54 us (18%)
  between operations  0.67 us (2%)
    pallas_call x1, Pallas kernels, shards(): pl.pallas_call(functools.partial(kernel, devices), out_shape=pltpu.VMEM((...  23.8 us
    unnamed x7, local copies, waits for them, and re-layouts  5.54 us

profile of v1, /device:TPU:14, one launch (start us, length us, event | category | flops | bytes accessed | tf_op | source)
XLA Modules:
  0.0 30.1 jit_solution(14117220361563370390)
XLA Ops:
  0.7 0.0 copy-start
  0.7 0.9 %copy-done = bf16[128,512]{1,0:T(8,128)(2,1)S(1)} copy-done((bf16[128,512]{1,0:T(8,128)(2,1)S(1)}, bf16[128,512]{1,0:T(8,128)(2,1)}, u32[]{:S(2)}) %copy-start) | copy-done | bytes 131096
  1.6 0.0 copy-start.1
  1.6 0.7 %copy-done.1 = bf16[65]{0:T(256)(128)(2,1)S(1)} copy-done((bf16[65]{0:T(256)(128)(2,1)S(1)}, bf16[65]{0:T(256)(128)(2,1)}, u32[]{:S(2)}) %copy-start.1) | copy-done | bytes 154
  2.2 0.0 copy-start.2
  2.2 0.7 %copy-done.2 = s32[1,9]{1,0:T(1,128)S(1)} copy-done((s32[1,9]{1,0:T(1,128)S(1)}, s32[1,9]{1,0:T(1,128)}, u32[]{:S(2)}) %copy-start.2) | copy-done | bytes 60
  2.9 23.8 %shard_map.46 = bf16[10,25,128,128]{3,2,1,0:T(8,128)(2,1)S(1)} custom-call(bf16[128,512]{1,0:T(8,128)(2,1)S(1)} %copy-done, bf16[1,65]{1,0:T(2,128)(2,1)S(1)} %bitcast.3, s32[1]{0:T(128)S(6)} %copy.7.live_count, s32[1,9]{1,0:T(1,128)S(1)} %copy-done.2), custom_call_target="tpu_custom_call" | custom-call | flops 4194304000 | bytes 8192000 | tf_op jit(solution)/shard_map/pallas_call | solution.py:283
  26.7 3.3 %copy.6 = bf16[128,10,25,128]{3,0,2,1:T(8,128)(2,1)} copy(bf16[128,10,25,128]{3,0,2,1:T(8,128)(2,1)S(1)} %bitcast.2) | data formatting | bytes 16384000
Async XLA Ops:
  0.7 0.9 %copy-start = (bf16[128,512]{1,0:T(8,128)(2,1)S(1)}, bf16[128,512]{1,0:T(8,128)(2,1)}, u32[]{:S(2)}) copy-start(bf16[128,512]{1,0:T(8,128)(2,1)} %records.1) | copy-start | bytes 393220
  1.6 0.7 %copy-start.1 = (bf16[65]{0:T(256)(128)(2,1)S(1)}, bf16[65]{0:T(256)(128)(2,1)}, u32[]{:S(2)}) copy-start(bf16[65]{0:T(256)(128)(2,1)} %param.5) | copy-start | bytes 394
  2.2 0.7 %copy-start.2 = (s32[1,9]{1,0:T(1,128)S(1)}, s32[1,9]{1,0:T(1,128)}, u32[]{:S(2)}) copy-start(s32[1,9]{1,0:T(1,128)} %pair_valid.1) | copy-start | bytes 112

commit v2 on v1

v2 whole, which is shorter than its diff:
```python
import functools

import jax
import jax.numpy as jnp
from jax import lax
from jax.experimental import pallas as pl
from jax.experimental.pallas import tpu as pltpu
from jax.sharding import PartitionSpec as P

HALF = 12
LAGS = 2 * HALF + 1
PARTS = 2
LANES = 128

epsilon = 1e-06

NT = (((1,), (1,)), ((), ()))
NN = (((1,), (0,)), ((), ()))


def split_squares(block):
    wide = block.astype(jnp.float32)
    square = wide * wide
    high = square.astype(jnp.bfloat16)
    low = (square - high.astype(jnp.float32)).astype(jnp.bfloat16)
    return high, low


def kernel(
    devices, records_in, taps_in, live_count, pair_valid_in, out,
    records, taps, pair_valid,
    held, shifted, spread, row_scale, scale,
    in_sem, z_sem, layer_sem, ten_sem, pair_sem, recv_sem,
):
    events, samples = records.shape
    reach = pair_valid.shape[1]
    half_taps = (taps.shape[1] - 1) // 2
    per_layer = (reach - 1) // 2
    far = reach - 1
    last = reach + 1
    chips = devices // 2
    me = lax.axis_index("ev")
    core = lax.rem(me, 2)
    chip = me // 2
    place = lax.rem(chip, per_layer)
    sibling = me + 1 - 2 * core

    def in_layer(d):
        return me - 2 * place + 2 * lax.rem(place + per_layer - d, per_layer)

    barrier = pltpu.get_barrier_semaphore()

    def greet(device):
        pl.semaphore_signal(
            barrier, inc=1, device_id=(device,), device_id_type=pl.DeviceIdType.MESH
        )

    inputs = [
        pltpu.make_async_copy(there, here, in_sem.at[i])
        for i, (there, here) in enumerate(
            [
                (taps_in, taps),
                (records_in, records),
                (pair_valid_in, pair_valid),
            ]
        )
    ]
    for copy in inputs:
        copy.start()

    has_down = chip >= per_layer
    has_up = chip + per_layer < chips
    across = {}
    for d in range(1, per_layer, 2):
        across[d] = (
            (place == d // 2) & has_down,
            (place == per_layer - 1 - d // 2) & (chip + d < chips),
        )
    greet(sibling)
    greeted = per_layer + has_down.astype(jnp.int32) + has_up.astype(jnp.int32)
    for d in range(1, per_layer):
        greet(in_layer(d))

    @pl.when(has_down)
    def _():
        greet(me - 2 * per_layer)

    @pl.when(has_up)
    def _():
        greet(me + 2 * per_layer)

    for d, (down, up) in across.items():
        greeted += down.astype(jnp.int32) + up.astype(jnp.int32)

        @pl.when(down)
        def _(d=d):
            greet(me - 2 * d)

        @pl.when(up)
        def _(d=d):
            greet(me + 2 * d)

    spread[...] = jnp.zeros_like(spread)
    inputs[0].wait()
    spread[0:1, 0 : taps.shape[1]] = taps[...].astype(jnp.float32)
    rolled = pltpu.roll(
        jnp.broadcast_to(spread[0:1, :], (samples, samples)),
        samples - half_taps, 1, stride=1, stride_axis=0,
    )
    t = lax.broadcasted_iota(jnp.int32, (samples, samples), 0)
    u = lax.broadcasted_iota(jnp.int32, (samples, samples), 1)
    band = jnp.where(jnp.abs(u - t) <= half_taps, rolled, 0.0).astype(jnp.bfloat16)
    row = lax.broadcasted_iota(jnp.int32, (events, samples), 0)
    inputs[1].wait()
    kept = jnp.where(row < live_count[0], records[...].astype(jnp.float32), 0.0)
    own = lax.dot_general(
        kept.astype(jnp.bfloat16), band, NT, preferred_element_type=jnp.float32
    ).astype(jnp.bfloat16)
    held[0] = own

    for k in range(1, last + 1):
        if k == last:
            missing = (core == 0) & (me + k >= devices)
        else:
            missing = me + k >= devices

        @pl.when(missing)
        def _(k=k):
            held[k] = jnp.zeros((events, samples), jnp.bfloat16)

    pl.semaphore_wait(barrier, greeted)

    def remote(source, slot, send_sem, device, part=None):
        rows = pl.ds(0, events)
        if part is not None:
            rows = pl.ds(part * (events // PARTS), events // PARTS)
        return pltpu.make_async_remote_copy(
            src_ref=held.at[source, rows],
            dst_ref=held.at[slot, rows],
            send_sem=send_sem,
            recv_sem=recv_sem.at[slot, part or 0],
            device_id=(device,),
            device_id_type=pl.DeviceIdType.MESH,
        )

    def arrived(slot, part):
        remote(slot, slot, z_sem.at[part or 0], sibling, part).wait_recv()

    def to_sibling(i):
        return remote(2 * i + 2 - 2 * core, 2 * i + 1, pair_sem.at[i], sibling)

    def sibling_wants(i):
        return 2 * chip + 2 * i + 2 - 2 * core < devices

    def z_copy(part):
        return remote(0, far, z_sem.at[part], me - 2 * per_layer, part)

    def across_copy(d, part):
        return remote(0, 2 * d, layer_sem.at[d - 1, part], me - 2 * d, part)

    def layer_copy(d, source, part):
        return remote(source, 2 * d, layer_sem.at[d - 1, part], in_layer(d), part)

    def relays(d):
        return has_up & (place < d) & (d != 2 * place + 1)

    def ten_copy(part):
        return remote(far, last, ten_sem.at[part], me - 2, part)

    @pl.when(has_down)
    def _():
        for part in range(PARTS):
            z_copy(part).start()

    for d, (down, up) in across.items():
        @pl.when(down)
        def _(d=d):
            for part in range(PARTS):
                across_copy(d, part).start()

    for d in range(per_layer - 1, 0, -1):
        @pl.when(place >= d)
        def _(d=d):
            for part in range(PARTS):
                layer_copy(d, 0, part).start()

    @pl.when(core == 1)
    def _():
        to_sibling(0).start()

    padded = jnp.concatenate(
        [own.astype(jnp.float32), jnp.zeros((events, LANES), jnp.float32)], axis=1
    )
    width = samples + LANES
    for lag in range(LAGS):
        moved = pltpu.roll(padded, (lag - HALF) % width, 1) if lag != HALF else padded
        shifted[lag] = moved[:, :samples].astype(jnp.bfloat16)
    ones = jnp.ones((samples, LANES), jnp.bfloat16)
    high, low = split_squares(own)
    row_scale[...] = lax.rsqrt(
        lax.dot_general(high, ones, NN, preferred_element_type=jnp.float32)
        + lax.dot_general(low, ones, NN, preferred_element_type=jnp.float32)
        + epsilon
    )

    def pass_far():
        for part in range(PARTS):
            @pl.when(has_up)
            def _(part=part):
                arrived(far, part)

            for d in range(per_layer - 1, 0, -1):
                @pl.when(relays(d))
                def _(d=d, part=part):
                    layer_copy(d, far, part).start()

            @pl.when((core == 0) & (chip >= 1) & has_up)
            def _(part=part):
                ten_copy(part).start()

        @pl.when((core == 0) & has_up)
        def _():
            to_sibling(far // 2 - 1).start()

        @pl.when((core == 1) & has_up)
        def _():
            to_sibling(far // 2).start()

    def pass_on(slot):
        @pl.when(2 * chip + slot < devices)
        def _():
            for part in range(PARTS):
                arrived(slot, part)

            @pl.when(core == 0)
            def _():
                to_sibling(slot // 2 - 1).start()

            @pl.when(core == 1)
            def _():
                to_sibling(slot // 2).start()

    def pass_last():
        @pl.when((core == 0) & (me + last < devices))
        def _():
            for part in range(PARTS):
                arrived(last, part)
            to_sibling(last // 2 - 1).start()

    def receive(slot):
        @pl.when(me + slot < devices)
        def _():
            arrived(slot, None)

    def correlate(slots):
        for i, slot in enumerate(slots):
            high, low = split_squares(held[slot])
            rows = jnp.ones((8, samples), jnp.bfloat16)
            total = lax.dot_general(rows, high, NT, preferred_element_type=jnp.float32)
            total += lax.dot_general(rows, low, NT, preferred_element_type=jnp.float32)
            partner_scale = lax.rsqrt(total + epsilon)
            if slot > 0:
                partner_scale *= pair_valid[0, slot - 1].astype(jnp.float32)
            scale[:, i * events : (i + 1) * events] = row_scale[...] * partner_scale[0:1, :]

        left = shifted[...].reshape(LAGS * events, samples)
        right = jnp.concatenate([held[slot] for slot in slots], axis=0)
        product = lax.dot_general(left, right, NT, preferred_element_type=jnp.float32)
        product = product.reshape(LAGS, events, len(slots) * events)
        product = (product * scale[...][None]).astype(jnp.bfloat16)
        for i, slot in enumerate(slots):
            out[slot] = product[:, :, i * events : (i + 1) * events]

    inputs[2].wait()
    pass_far()
    correlate((0, far))
    evens = list(range(2, far, 2))
    ready = []
    for slot in evens:
        pass_on(slot)
        ready.append(slot)
        if len(ready) == 2:
            correlate(tuple(ready))
            ready = []
    pass_last()
    for slot in range(1, reach + 1, 2):
        receive(slot)
        ready.append(slot)
        if len(ready) == 2:
            correlate(tuple(ready))
            ready = []

    for part in range(PARTS):
        @pl.when(has_down)
        def _(part=part):
            z_copy(part).wait_send()

        for d in range(1, per_layer):
            @pl.when((place >= d) | relays(d))
            def _(d=d, part=part):
                layer_copy(d, 0, part).wait_send()

        for d, (down, up) in across.items():
            @pl.when(down)
            def _(d=d, part=part):
                across_copy(d, part).wait_send()

        @pl.when((core == 0) & (chip >= 1) & has_up)
        def _(part=part):
            ten_copy(part).wait_send()

    for i in range((reach + 1) // 2):
        @pl.when(sibling_wants(i))
        def _(i=i):
            to_sibling(i).wait_send()


def shards(devices, records, filter_taps, live_counts, pair_valid):
    events, samples = records.shape
    reach = pair_valid.shape[1]
    vmem = pl.BlockSpec(memory_space=pltpu.VMEM)
    hbm = pl.BlockSpec(memory_space=pltpu.HBM)
    taps = filter_taps.reshape(1, -1)
    records, taps, pair_valid = [
        pltpu.with_memory_space_constraint(x, pltpu.HBM)
        for x in (records, taps, pair_valid)
    ]
    correlations = pl.pallas_call(
        functools.partial(kernel, devices),
        out_shape=pltpu.VMEM((reach + 1, LAGS, events, events), jnp.bfloat16),
        in_specs=[hbm, hbm, pl.BlockSpec(memory_space=pltpu.SMEM), hbm],
        out_specs=vmem,
        scratch_shapes=[
            pltpu.VMEM((events, samples), jnp.bfloat16),
            pltpu.VMEM((1, filter_taps.shape[0]), jnp.bfloat16),
            pltpu.SMEM((1, reach), jnp.int32),
            pltpu.VMEM((reach + 2, events, samples), jnp.bfloat16),
            pltpu.VMEM((LAGS, events, samples), jnp.bfloat16),
            pltpu.VMEM((8, samples), jnp.float32),
            pltpu.VMEM((events, LANES), jnp.float32),
            pltpu.VMEM((events, 2 * events), jnp.float32),
            pltpu.SemaphoreType.DMA((3,)),
            pltpu.SemaphoreType.DMA((PARTS,)),
            pltpu.SemaphoreType.DMA(((reach - 1) // 2 - 1, PARTS)),
            pltpu.SemaphoreType.DMA((PARTS,)),
            pltpu.SemaphoreType.DMA(((reach + 1) // 2,)),
            pltpu.SemaphoreType.DMA((reach + 2, PARTS)),
        ],
        compiler_params=pltpu.CompilerParams(
            collective_id=0, has_side_effects=True, vmem_limit_bytes=40 * 1024 * 1024
        ),
        cost_estimate=pl.CostEstimate(
            flops=2 * (reach + 1) * LAGS * events * events * samples,
            bytes_accessed=2 * (reach + 1) * LAGS * events * events,
            transcendentals=0,
        ),
    )(records, taps, live_counts, pair_valid)
    return jnp.transpose(correlations, (2, 0, 1, 3))


def solution(mesh):
    in_specs = (P("ev", None), P(), P("ev"), P("ev", None))
    out_specs = P("ev", None, None, None)
    return jax.shard_map(
        functools.partial(shards, mesh.shape["ev"]),
        mesh=mesh, in_specs=in_specs, out_specs=out_specs, check_vma=False,
    )
```

time: 30.2 us -> 25.4 us (0.84)
  Pallas kernels: 23.8 us -> 21.3 us
  local copies, waits for them, and re-layouts: 5.54 us -> 3.33 us
    pallas_call x1, Pallas kernels: 23.8 us -> 21.3 us  [shards(): pl.pallas_call(functools.partial(kernel, devices), out_shape=pltpu.VMEM((...]
    unnamed x7 -> x1, local copies, waits for them, and re-layouts: 5.54 us -> 3.33 us
where the time goes in v2:
time: 25.4 us; the launch traced here: 25.3 us
  Pallas kernels  21.3 us (84%)
  local copies, waits for them, and re-layouts  3.33 us (13%)
  between operations  0.66 us (3%)
    pallas_call x1, Pallas kernels, shards(): pl.pallas_call(functools.partial(kernel, devices), out_shape=pltpu.VMEM((...  21.3 us
    unnamed x1, local copies, waits for them, and re-layouts  3.33 us

profile of v2, /device:TPU:14, one launch (start us, length us, event | category | flops | bytes accessed | tf_op | source)
XLA Modules:
  0.0 25.3 jit_solution(2083515700895481396)
XLA Ops:
  0.7 21.3 %shard_map.46 = bf16[10,25,128,128]{3,2,1,0:T(8,128)(2,1)S(1)} custom-call(bf16[128,512]{1,0:T(8,128)(2,1)} %records_in.1, bf16[1,65]{1,0:T(2,128)(2,1)} %bitcast.3, s32[1]{0:T(128)S(6)} %copy.7.live_count, s32[1,9]{1,0:T(1,128)} %pair_valid_in.1), custom_call_target="tpu_custom_call" | custom-call | flops 4194304000 | bytes 8192000 | tf_op jit(solution)/shard_map/pallas_call | solution.py:328
  21.9 3.3 %copy.6 = bf16[128,10,25,128]{3,0,2,1:T(8,128)(2,1)} copy(bf16[128,10,25,128]{3,0,2,1:T(8,128)(2,1)S(1)} %bitcast.2) | data formatting | bytes 16384000

commit v3 on v2

--- a/solution.py
+++ b/solution.py
@@ -26,10 +26,47 @@
     return high, low
 
 
+def in_order(reach):
+    order = [0, reach - 1, *range(2, reach - 1, 2), *range(1, reach + 1, 2)]
+    pairs = [tuple(order[i : i + 2]) for i in range(0, len(order), 2)]
+    return pairs[:-2], pairs[-2:]
+
+
+def product_of(shifted, right, scale):
+    lags, events, samples = shifted.shape
+    left = shifted[...].reshape(lags * events, samples)
+    product = lax.dot_general(left, right, NT, preferred_element_type=jnp.float32)
+    return (product.reshape(lags, events, -1) * scale[None]).astype(jnp.bfloat16)
+
+
+def finish(first, second, done, shifted, late, late_scale, out, fresh, sems):
+    events = shifted.shape[1]
+    copies = []
+
+    def send(source, slot):
+        copy = pltpu.make_async_copy(source, out.at[slot], sems.at[len(copies)])
+        copy.start()
+        copies.append(copy)
+
+    for n, slot in enumerate(sum(first, ())):
+        send(done.at[n], slot)
+    n = 0
+    for i, slots in enumerate(second):
+        right = late[n : n + len(slots)].reshape(len(slots) * events, -1)
+        product = product_of(shifted, right, late_scale[i])
+        for j, slot in enumerate(slots):
+            fresh[n] = product[:, :, j * events : (j + 1) * events]
+            send(fresh.at[n], slot)
+            n += 1
+    for copy in copies:
+        copy.wait()
+
+
 def kernel(
-    devices, records_in, taps_in, live_count, pair_valid_in, out,
+    devices, records_in, taps_in, live_count, pair_valid_in,
+    done, shifted, late, late_scale,
     records, taps, pair_valid,
-    held, shifted, spread, row_scale, scale,
+    held, spread, row_scale,
     in_sem, z_sem, layer_sem, ten_sem, pair_sem, recv_sem,
 ):
     events, samples = records.shape
@@ -252,8 +289,9 @@
         def _():
             arrived(slot, None)
 
-    def correlate(slots):
-        for i, slot in enumerate(slots):
+    def scale_of(slots):
+        parts = []
+        for slot in slots:
             high, low = split_squares(held[slot])
             rows = jnp.ones((8, samples), jnp.bfloat16)
             total = lax.dot_general(rows, high, NT, preferred_element_type=jnp.float32)
@@ -261,34 +299,40 @@
             partner_scale = lax.rsqrt(total + epsilon)
             if slot > 0:
                 partner_scale *= pair_valid[0, slot - 1].astype(jnp.float32)
-            scale[:, i * events : (i + 1) * events] = row_scale[...] * partner_scale[0:1, :]
-
-        left = shifted[...].reshape(LAGS * events, samples)
+            parts.append(row_scale[...] * partner_scale[0:1, :])
+        return jnp.concatenate(parts, axis=1)
+
+    first, second = in_order(reach)
+    inputs[2].wait()
+
+    def await_slot(slot):
+        if slot == 0:
+            return
+        if slot == far:
+            pass_far()
+        elif slot % 2 == 0:
+            pass_on(slot)
+            if slot == far - 2:
+                pass_last()
+        else:
+            receive(slot)
+
+    n = 0
+    for slots in first:
+        for slot in slots:
+            await_slot(slot)
         right = jnp.concatenate([held[slot] for slot in slots], axis=0)
-        product = lax.dot_general(left, right, NT, preferred_element_type=jnp.float32)
-        product = product.reshape(LAGS, events, len(slots) * events)
-        product = (product * scale[...][None]).astype(jnp.bfloat16)
-        for i, slot in enumerate(slots):
-            out[slot] = product[:, :, i * events : (i + 1) * events]
-
-    inputs[2].wait()
-    pass_far()
-    correlate((0, far))
-    evens = list(range(2, far, 2))
-    ready = []
-    for slot in evens:
-        pass_on(slot)
-        ready.append(slot)
-        if len(ready) == 2:
-            correlate(tuple(ready))
-            ready = []
-    pass_last()
-    for slot in range(1, reach + 1, 2):
-        receive(slot)
-        ready.append(slot)
-        if len(ready) == 2:
-            correlate(tuple(ready))
-            ready = []
+        product = product_of(shifted, right, scale_of(slots))
+        for i in range(len(slots)):
+            done[n] = product[:, :, i * events : (i + 1) * events]
+            n += 1
+    n = 0
+    for i, slots in enumerate(second):
+        for slot in slots:
+            await_slot(slot)
+            late[n] = held[slot]
+            n += 1
+        late_scale[i] = scale_of(slots)
 
     for part in range(PARTS):
         @pl.when(has_down)
@@ -325,20 +369,26 @@
         pltpu.with_memory_space_constraint(x, pltpu.HBM)
         for x in (records, taps, pair_valid)
     ]
-    correlations = pl.pallas_call(
+    first, second = in_order(reach)
+    done_count = sum(len(slots) for slots in first)
+    late_count = sum(len(slots) for slots in second)
+    arrays = pl.pallas_call(
         functools.partial(kernel, devices),
-        out_shape=pltpu.VMEM((reach + 1, LAGS, events, events), jnp.bfloat16),
+        out_shape=[
+            pltpu.VMEM((done_count, LAGS, events, events), jnp.bfloat16),
+            pltpu.VMEM((LAGS, events, samples), jnp.bfloat16),
+            pltpu.VMEM((late_count, events, samples), jnp.bfloat16),
+            pltpu.VMEM((len(second), events, 2 * events), jnp.float32),
+        ],
         in_specs=[hbm, hbm, pl.BlockSpec(memory_space=pltpu.SMEM), hbm],
-        out_specs=vmem,
+        out_specs=[vmem] * 4,
         scratch_shapes=[
             pltpu.VMEM((events, samples), jnp.bfloat16),
             pltpu.VMEM((1, filter_taps.shape[0]), jnp.bfloat16),
             pltpu.SMEM((1, reach), jnp.int32),
             pltpu.VMEM((reach + 2, events, samples), jnp.bfloat16),
-            pltpu.VMEM((LAGS, events, samples), jnp.bfloat16),
             pltpu.VMEM((8, samples), jnp.float32),
             pltpu.VMEM((events, LANES), jnp.float32),
-            pltpu.VMEM((events, 2 * events), jnp.float32),
             pltpu.SemaphoreType.DMA((3,)),
             pltpu.SemaphoreType.DMA((PARTS,)),
             pltpu.SemaphoreType.DMA(((reach - 1) // 2 - 1, PARTS)),
@@ -347,7 +397,7 @@
             pltpu.SemaphoreType.DMA((reach + 2, PARTS)),
         ],
         compiler_params=pltpu.CompilerParams(
-            collective_id=0, has_side_effects=True, vmem_limit_bytes=40 * 1024 * 1024
+            collective_id=0, has_side_effects=True, vmem_limit_bytes=24 * 1024 * 1024
         ),
         cost_estimate=pl.CostEstimate(
             flops=2 * (reach + 1) * LAGS * events * events * samples,
@@ -355,6 +405,17 @@
             transcendentals=0,
         ),
     )(records, taps, live_counts, pair_valid)
+    correlations = pl.pallas_call(
+        functools.partial(finish, first, second),
+        out_shape=jax.ShapeDtypeStruct((reach + 1, LAGS, events, events), jnp.bfloat16),
+        in_specs=[vmem] * 4,
+        out_specs=hbm,
+        scratch_shapes=[
+            pltpu.VMEM((late_count, LAGS, events, events), jnp.bfloat16),
+            pltpu.SemaphoreType.DMA((reach + 1,)),
+        ],
+        compiler_params=pltpu.CompilerParams(vmem_limit_bytes=24 * 1024 * 1024),
+    )(*arrays)
     return jnp.transpose(correlations, (2, 0, 1, 3))
 
 

time: 25.4 us -> 21.9 us (0.86)
  local copies, waits for them, and re-layouts: 3.33 us -> 0 us
    unnamed x1 -> x0, local copies, waits for them, and re-layouts: 3.33 us -> none
    pallas_call x1 -> x2, Pallas kernels: 21.3 us -> 21.1 us  [the longest x1 17.5 us: shards(): pl.pallas_call(functools.partial(kernel, devices), out_shape=[pltpu.VMEM(...]
where the time goes in v3:
time: 21.9 us; the launch traced here: 21.8 us
  Pallas kernels  21.1 us (96%)
  between operations  0.66 us (3%)
    pallas_call x1, Pallas kernels, shards(): pl.pallas_call(functools.partial(kernel, devices), out_shape=[pltpu.VMEM(...  17.5 us
    pallas_call x1, Pallas kernels, shards(): pl.pallas_call(functools.partial(finish, first, second), out_shape=jax.Sh...  3.62 us

profile of v3, /device:TPU:14, one launch (start us, length us, event | category | flops | bytes accessed | tf_op | source)
XLA Modules:
  0.0 21.8 jit_solution(7914665410684546907)
XLA Ops:
  0.7 17.5 %shard_map.46 = (bf16[6,25,128,128]{3,2,1,0:T(8,128)(2,1)S(1)}, bf16[25,128,512]{2,1,0:T(8,128)(2,1)S(1)}, bf16[4,128,512]{2,1,0:T(8,128)(2,1)S(1)}, f32[2,128,256]{2,1,0:T(8,128)S(1)}) custom-call(bf16[128,512]{1,0:T(8,128)(2,1)} %records_in.1, bf16[1,65]{1,0:T(2,128)(2,1)} %bitcast.2, s32[1]{0:T(128)S(6)} %copy.5.live_count, s32[1,9]{1,0:T(1,128)} %pair_valid_in.1), custom_call_target="tpu_custom_call" | custom-call | flops 4194304000 | bytes 8192000 | tf_op jit(solution)/shard_map/pallas_call | solution.py:375
  18.1 3.6 %shard_map.47 = bf16[10,25,128,128]{3,2,1,0:T(8,128)(2,1)} custom-call(bf16[6,25,128,128]{3,2,1,0:T(8,128)(2,1)S(1)} %get-tuple-element.9.done, bf16[25,128,512]{2,1,0:T(8,128)(2,1)S(1)} %get-tuple-element.10.shifted, bf16[4,128,512]{2,1,0:T(8,128)(2,1)S(1)} %get-tuple-element.11.late, f32[2,128,256]{2,1,0:T(8,128)S(1)} %get-tuple-element.12.late_scale), custom_call_target="tpu_custom_call" | custom-call | tf_op jit(solution)/shard_map/pallas_call | solution.py:408

commit v4 on v3

--- a/solution.py
+++ b/solution.py
@@ -9,7 +9,7 @@
 
 HALF = 12
 LAGS = 2 * HALF + 1
-PARTS = 2
+PARTS = 4
 LANES = 128
 
 epsilon = 1e-06

time: 21.9 us -> 21.8 us (level)
  no operation moved by 1% of the time
where the time goes in v4:
time: 21.8 us; the launch traced here: 21.7 us
  Pallas kernels  21 us (96%)
  between operations  0.66 us (3%)
    pallas_call x1, Pallas kernels, shards(): pl.pallas_call(functools.partial(kernel, devices), out_shape=[pltpu.VMEM(...  17.4 us
    pallas_call x1, Pallas kernels, shards(): pl.pallas_call(functools.partial(finish, first, second), out_shape=jax.Sh...  3.63 us

profile of v4, /device:TPU:14, one launch (start us, length us, event | category | flops | bytes accessed | tf_op | source)
XLA Modules:
  0.0 21.7 jit_solution(13571550463959015822)
XLA Ops:
  0.7 17.4 %shard_map.46 = (bf16[6,25,128,128]{3,2,1,0:T(8,128)(2,1)S(1)}, bf16[25,128,512]{2,1,0:T(8,128)(2,1)S(1)}, bf16[4,128,512]{2,1,0:T(8,128)(2,1)S(1)}, f32[2,128,256]{2,1,0:T(8,128)S(1)}) custom-call(bf16[128,512]{1,0:T(8,128)(2,1)} %records_in.1, bf16[1,65]{1,0:T(2,128)(2,1)} %bitcast.2, s32[1]{0:T(128)S(6)} %copy.5.live_count, s32[1,9]{1,0:T(1,128)} %pair_valid_in.1), custom_call_target="tpu_custom_call" | custom-call | flops 4194304000 | bytes 8192000 | tf_op jit(solution)/shard_map/pallas_call | solution.py:375
  18.1 3.6 %shard_map.47 = bf16[10,25,128,128]{3,2,1,0:T(8,128)(2,1)} custom-call(bf16[6,25,128,128]{3,2,1,0:T(8,128)(2,1)S(1)} %get-tuple-element.9.done, bf16[25,128,512]{2,1,0:T(8,128)(2,1)S(1)} %get-tuple-element.10.shifted, bf16[4,128,512]{2,1,0:T(8,128)(2,1)S(1)} %get-tuple-element.11.late, f32[2,128,256]{2,1,0:T(8,128)S(1)} %get-tuple-element.12.late_scale), custom_call_target="tpu_custom_call" | custom-call | tf_op jit(solution)/shard_map/pallas_call | solution.py:408
